TPU v7x, 32 devices: a whole 2x2x4 slice. The times are simulated.
32 devices in a mesh: band: 4 (over y, x), dev: 8 (over z, core).
Axes of the slice: x: 2, y: 2, z: 4, core: 2. Of those that a mesh axis runs over, the one named last changes fastest.
Arguments:
- drive: float32 [2, 32, 16384], P(None, None, ('band', 'dev')), may hold values from -6 to 6
- coords: float32 [3, 16384], P(None, ('band', 'dev')), may hold values from 0 to 3
- rule_index: int32 [16384], P(('band', 'dev')), may hold values from 0 to 3
- rule_weight: float32 [4], replicated, may hold values from 0.1 to 0.4
- pair_cols: int32 [3072], P(('band', 'dev')), may hold values from 0 to 63, as said below
- pair_count: int32 [32], P(('band', 'dev')), may hold values from 12 to 96, as said below
Outputs:
- near_field: float32 [2, 32, 16384], P(None, None, ('band', 'dev'))
Inputs may be any that keep to these rules, and one draw needn't show every extreme that they name: `pair_cols`: for slot s of device k the listed block column lies from k * 2 + (s mod 2) up to that row plus 16 - 1; slots s < 2 list the diagonal pair. `pair_count`: some device has all 96 slots live.
All inputs are finite; a program needn't handle non-finite values.
Results may differ from a plain program's by a relative error of at most 0.0003.
Values sent between devices are 32-bit elements; how exact they have to be, the bound alone decides.
No kernel may reach another device: no remote copies, remote signals or barrier semaphores. Data moves between devices by JAX's collectives and lax.ppermute only.
A program may use at most 64 MiB of HBM per device.

v0:
```python
import math

import jax
import jax.numpy as jnp
from jax import lax
from jax.sharding import PartitionSpec as P

BLOCK = 256
RULES = 4
BR_DEV = 2
TILE_DEV = 96


wave_number = 25.0
smoothing = 0.05
highest = lax.Precision.HIGHEST


def from_behind(value, axis, steps):
    count = lax.axis_size(axis)
    initial, last = (max(0, -steps), min(count, count - steps))
    return lax.ppermute(value, axis, [(source, source + steps) for source in range(initial, last)])


def point_weights(rule_index, rule_weight):
    matches = rule_index[:, None] == jnp.arange(RULES, dtype=jnp.int32)[None, :]
    return jnp.sum(
        jnp.where(matches, rule_weight[None, :], jnp.zeros_like(rule_weight)[None, :]), axis=1
    )


def assemble(near_points, far_points, near_w, far_w):
    offsets = near_points[:, :, None] - far_points[:, None, :]
    distance = jnp.sqrt(jnp.sum(offsets * offsets, axis=0) + smoothing * smoothing)
    strength = near_w[:, None] * far_w[None, :] / (4.0 * math.pi * distance)
    phases = wave_number * distance
    return (strength * jnp.cos(phases), strength * jnp.sin(phases))


def batch_apply(vectors, real_part, imag_part, form):
    real_prod = jnp.einsum(
        form, vectors, real_part, precision=highest, preferred_element_type=jnp.float32
    )
    imag_prod = jnp.einsum(
        form, vectors, imag_part, precision=highest, preferred_element_type=jnp.float32
    )
    return jnp.stack([real_prod[:, 0] - imag_prod[:, 1], real_prod[:, 1] + imag_prod[:, 0]], axis=1)


def add_block(accumulated, update_block, block_index):
    previous = lax.dynamic_slice_in_dim(accumulated, block_index * BLOCK, BLOCK, 2)
    return lax.dynamic_update_slice_in_dim(
        accumulated, previous + update_block, block_index * BLOCK, 2
    )


def body(drive, coords, rule_index, rule_weight, pair_cols, pair_count):
    n_dev = lax.axis_size("dev")
    band_index = lax.axis_index("band")
    dev_index = lax.axis_index("dev")
    patterns = drive.shape[1]
    own_cols = drive.shape[2]
    band_cols = n_dev * own_cols
    weights = point_weights(rule_index, rule_weight)
    geometry = jnp.concatenate([coords, weights[None, :]], axis=0)
    band_rows = n_dev * BR_DEV
    band_first = band_index * band_rows
    band_x, band_g = (
        lax.all_gather(drive, "dev", axis=2, tiled=True),
        lax.all_gather(geometry, "dev", axis=1, tiled=True),
    )
    next_x, next_g = from_behind((band_x, band_g), "band", -1)
    window_x = jnp.concatenate([band_x, next_x], axis=2)
    window_g = jnp.concatenate([band_g, next_g], axis=1)
    all_cols, all_counts = (
        lax.all_gather(pair_cols, "dev", axis=0, tiled=True),
        lax.all_gather(pair_count, "dev", axis=0, tiled=True),
    )
    slot_ids = jnp.arange(n_dev * TILE_DEV, dtype=jnp.int32)
    owner_dev = slot_ids // TILE_DEV
    local_slot = slot_ids % TILE_DEV
    owner_match = owner_dev[:, None] == jnp.arange(n_dev, dtype=jnp.int32)[None, :]
    slot_counts = jnp.sum(jnp.where(owner_match, all_counts[None, :], 0), axis=1)
    is_live = local_slot < slot_counts
    live_rank = jnp.cumsum(is_live.astype(jnp.int32)) - 1
    live_total = jnp.sum(is_live.astype(jnp.int32))
    wanted = jnp.arange(TILE_DEV, dtype=jnp.int32) * n_dev + dev_index
    matches = (live_rank[None, :] == wanted[:, None]) & is_live[None, :]
    slot_rows = owner_dev * BR_DEV + local_slot % BR_DEV
    tile_rows = jnp.sum(jnp.where(matches, slot_rows[None, :], 0), axis=1)
    tile_cols = jnp.sum(jnp.where(matches, all_cols[None, :] - band_first, 0), axis=1)
    live_tiles = (live_total - dev_index + n_dev - 1) // n_dev
    per_turn = 8
    turns = (live_tiles + per_turn - 1) // per_turn

    def one_turn(turn_index, accumulated):
        first_slot = turn_index * per_turn
        pick_rows = lax.dynamic_slice_in_dim(tile_rows, first_slot, per_turn, 0)
        pick_cols = lax.dynamic_slice_in_dim(tile_cols, first_slot, per_turn, 0)
        slot_ids = first_slot + jnp.arange(per_turn, dtype=jnp.int32)
        keep_mask = (slot_ids < live_tiles).astype(jnp.float32)
        mirror = keep_mask * (pick_rows != pick_cols).astype(jnp.float32)
        near_x = jnp.stack(
            [
                lax.dynamic_slice_in_dim(window_x, pick_rows[g] * BLOCK, BLOCK, 2)
                for g in range(per_turn)
            ]
        )
        far_x = jnp.stack(
            [
                lax.dynamic_slice_in_dim(window_x, pick_cols[g] * BLOCK, BLOCK, 2)
                for g in range(per_turn)
            ]
        )
        near_g = jnp.stack(
            [
                lax.dynamic_slice_in_dim(window_g, pick_rows[g] * BLOCK, BLOCK, 1)
                for g in range(per_turn)
            ]
        )
        far_g = jnp.stack(
            [
                lax.dynamic_slice_in_dim(window_g, pick_cols[g] * BLOCK, BLOCK, 1)
                for g in range(per_turn)
            ]
        )
        real_part, imag_part = jax.vmap(assemble)(
            near_g[:, :3], far_g[:, :3], near_g[:, 3], far_g[:, 3]
        )
        direct = (
            batch_apply(far_x, real_part, imag_part, "tcrq,tpq->tcrp")
            * keep_mask[:, None, None, None]
        )
        mirrored = (
            batch_apply(near_x, real_part, imag_part, "tcrp,tpq->tcrq")
            * mirror[:, None, None, None]
        )
        for g in range(per_turn):
            accumulated = add_block(accumulated, direct[g], pick_rows[g])
            accumulated = add_block(accumulated, mirrored[g], pick_cols[g])
        return accumulated

    accumulated = jnp.zeros((2, patterns, 2 * band_cols), jnp.float32)
    accumulated = lax.fori_loop(0, turns, one_turn, accumulated)
    own_part = accumulated[:, :, :band_cols]
    next_part = accumulated[:, :, band_cols:]
    carried = from_behind(next_part, "band", 1)
    return lax.psum_scatter(own_part + carried, "dev", scatter_dimension=2, tiled=True)


def solution(mesh):
    in_specs = (
        P(None, None, ("band", "dev")),
        P(None, ("band", "dev")),
        P(("band", "dev")),
        P(),
        P(("band", "dev")),
        P(("band", "dev")),
    )
    out_specs = P(None, None, ("band", "dev"))
    return jax.shard_map(body, mesh=mesh, in_specs=in_specs, out_specs=out_specs, check_vma=False)
```

profile of v0, /device:TPU:0, one launch (start us, length us, event | category | flops | bytes accessed | tf_op | source)
XLA Modules:
  0.0 578.0 jit_solution(12796849646930328614)
XLA Ops:
  8.0 1.2 dynamic-slice
  12.9 15.6 %all_gather.15 = f32[4,4096]{1,0:T(4,128)S(1)} all-gather(f32[4,512]{1,0:T(4,128)S(1)} %pad_maximum_fusion.2), channel_id=1, replica_groups=mesh['band'=4,'dev'=8] {'dev'}, dimensions={1}, use_global_device_ids=true | all-gather | bytes 73728 | tf_op jit(solution)/shard_map/all_gather | solution.py:70
  28.6 1.3 collective-permute-start.1
  29.9 9.1 %all-reduce.2 = (s32[8]{0:T(128)S(1)}, s32[768]{0:T(1024)S(1)}) all-reduce(s32[8]{0:T(128)S(1)} %dynamic-update-slice, s32[768]{0:T(1024)S(1)} %dynamic-update-slice.1), channel_id=1, replica_groups=mesh['band'=4,'dev'=8] {'dev'}, use_global_device_ids=true, to_apply=%add | all-reduce | flops 776 | bytes 6208
  40.4 1.3 collective-permute-start
  42.7 24.1 %collective-permute-done = f32[2,32,4096]{2,1,0:T(8,128)S(1)} collective-permute-done((f32[2,32,4096]{2,1,0:T(8,128)}, f32[2,32,4096]{2,1,0:T(8,128)S(1)}, u32[]{:S(2)}, u32[]{:S(2)}) %collective-permute-start) | collective-permute-done | bytes 1048608 | tf_op jit(solution)/shard_map/ppermute | solution.py:22
  66.8 2.7 pad_maximum_fusion
  69.7 382.1 %while.10 = (s32[]{:T(128)}, f32[2,32,8192]{2,1,0:T(8,128)S(1)}, s32[]{:T(128)}, s32[96]{0:T(128)S(1)}, s32[96]{0:T(128)S(1)}, /*index=5*/f32[2,32,8192]{2,1,0:T...) while((s32[]{:T(128)}, f32[2,32,8192]{2,1,0:T(8,128)S(1)}, ...), condition=%wide.region_9.10_spmd, body=%wide.region_7.9_spmd.sunk | while | flops 1628438656 | bytes 25904608 | solution.py:144
  85.1 0.9 bitcast_dynamic-update-slice_fusion.28
  86.0 0.9 bitcast_dynamic-update-slice_fusion.29
  88.7 1.1 multiply_reduce_fusion.2
  89.8 10.4 %fusion.103 = f32[8,2,32,256]{3,2,1,0:T(8,128)S(1)} fusion(f32[8,2,32,256]{3,2,1,0:T(8,128)S(1)} %get-tuple-element.291, f32[8,256,256]{2,1,0:T(8,128)S(1)} %multiply_reduce_fusion.2, f32[8,256]{1,0:T(8,128)S(1)} %slice_bitcast_fusion.20, f32[8,256]{1,0:T(8,128)S(1)} %slice_bitcast_fusion.21), kind=kOutput, calls=%fused_computation.5.clone.1 | convolution fusion | flops 405798912 | bytes 3162112 | tf_op jit(solution)/shard_map/while/body/tcrp,tpq->tcrq/dot_general | solution.py:41
  100.3 10.6 %fusion.102 = f32[8,2,32,256]{3,2,1,0:T(8,128)S(1)} fusion(f32[8,2,32,256]{3,2,1,0:T(8,128)S(1)} %get-tuple-element.291, f32[8,256,256]{2,1,0:T(8,128)S(1)} %multiply_reduce_fusion.2, f32[8,256]{1,0:T(8,128)S(1)} %slice_bitcast_fusion.20, f32[8,256]{1,0:T(8,128)S(1)} %slice_bitcast_fusion.21), kind=kOutput, calls=%fused_computation.1.clone.1 | convolution fusion | flops 405798912 | bytes 3162112 | tf_op jit(solution)/shard_map/while/body/tcrp,tpq->tcrq/dot_general | solution.py:44
  110.9 10.8 %fusion.101 = f32[8,2,32,256]{3,2,1,0:T(8,128)S(1)} fusion(f32[8,2,32,256]{3,2,1,0:T(8,128)S(1)} %get-tuple-element.270, f32[8,256,256]{2,1,0:T(8,128)S(1)} %multiply_reduce_fusion.2, f32[8,256]{1,0:T(8,128)S(1)} %slice_bitcast_fusion.20, f32[8,256]{1,0:T(8,128)S(1)} %slice_bitcast_fusion.21), kind=kOutput, calls=%fused_computation.7.clone.1 | convolution fusion | flops 405798912 | bytes 3162112 | tf_op jit(solution)/shard_map/while/body/tcrq,tpq->tcrp/dot_general | solution.py:41
  121.8 10.9 %fusion.100 = f32[8,2,32,256]{3,2,1,0:T(8,128)S(1)} fusion(f32[8,2,32,256]{3,2,1,0:T(8,128)S(1)} %get-tuple-element.270, f32[8,256,256]{2,1,0:T(8,128)S(1)} %multiply_reduce_fusion.2, f32[8,256]{1,0:T(8,128)S(1)} %slice_bitcast_fusion.20, f32[8,256]{1,0:T(8,128)S(1)} %slice_bitcast_fusion.21), kind=kOutput, calls=%fused_computation.3.clone.1 | convolution fusion | flops 405798912 | bytes 3162112 | tf_op jit(solution)/shard_map/while/body/tcrq,tpq->tcrp/dot_general | solution.py:44
  149.7 0.9 bitcast_dynamic-update-slice_fusion.29
  152.4 1.1 multiply_reduce_fusion.2
  153.5 10.4 %fusion.103 = f32[8,2,32,256]{3,2,1,0:T(8,128)S(1)} fusion(f32[8,2,32,256]{3,2,1,0:T(8,128)S(1)} %get-tuple-element.291, f32[8,256,256]{2,1,0:T(8,128)S(1)} %multiply_reduce_fusion.2, f32[8,256]{1,0:T(8,128)S(1)} %slice_bitcast_fusion.20, f32[8,256]{1,0:T(8,128)S(1)} %slice_bitcast_fusion.21), kind=kOutput, calls=%fused_computation.5.clone.1 | convolution fusion | flops 405798912 | bytes 3162112 | tf_op jit(solution)/shard_map/while/body/tcrp,tpq->tcrq/dot_general | solution.py:41
  164.0 10.6 %fusion.102 = f32[8,2,32,256]{3,2,1,0:T(8,128)S(1)} fusion(f32[8,2,32,256]{3,2,1,0:T(8,128)S(1)} %get-tuple-element.291, f32[8,256,256]{2,1,0:T(8,128)S(1)} %multiply_reduce_fusion.2, f32[8,256]{1,0:T(8,128)S(1)} %slice_bitcast_fusion.20, f32[8,256]{1,0:T(8,128)S(1)} %slice_bitcast_fusion.21), kind=kOutput, calls=%fused_computation.1.clone.1 | convolution fusion | flops 405798912 | bytes 3162112 | tf_op jit(solution)/shard_map/while/body/tcrp,tpq->tcrq/dot_general | solution.py:44
  174.6 10.8 %fusion.101 = f32[8,2,32,256]{3,2,1,0:T(8,128)S(1)} fusion(f32[8,2,32,256]{3,2,1,0:T(8,128)S(1)} %get-tuple-element.270, f32[8,256,256]{2,1,0:T(8,128)S(1)} %multiply_reduce_fusion.2, f32[8,256]{1,0:T(8,128)S(1)} %slice_bitcast_fusion.20, f32[8,256]{1,0:T(8,128)S(1)} %slice_bitcast_fusion.21), kind=kOutput, calls=%fused_computation.7.clone.1 | convolution fusion | flops 405798912 | bytes 3162112 | tf_op jit(solution)/shard_map/while/body/tcrq,tpq->tcrp/dot_general | solution.py:41
  185.5 10.9 %fusion.100 = f32[8,2,32,256]{3,2,1,0:T(8,128)S(1)} fusion(f32[8,2,32,256]{3,2,1,0:T(8,128)S(1)} %get-tuple-element.270, f32[8,256,256]{2,1,0:T(8,128)S(1)} %multiply_reduce_fusion.2, f32[8,256]{1,0:T(8,128)S(1)} %slice_bitcast_fusion.20, f32[8,256]{1,0:T(8,128)S(1)} %slice_bitcast_fusion.21), kind=kOutput, calls=%fused_computation.3.clone.1 | convolution fusion | flops 405798912 | bytes 3162112 | tf_op jit(solution)/shard_map/while/body/tcrq,tpq->tcrp/dot_general | solution.py:44
  216.0 1.1 multiply_reduce_fusion.2
  217.1 10.4 %fusion.103 = f32[8,2,32,256]{3,2,1,0:T(8,128)S(1)} fusion(f32[8,2,32,256]{3,2,1,0:T(8,128)S(1)} %get-tuple-element.291, f32[8,256,256]{2,1,0:T(8,128)S(1)} %multiply_reduce_fusion.2, f32[8,256]{1,0:T(8,128)S(1)} %slice_bitcast_fusion.20, f32[8,256]{1,0:T(8,128)S(1)} %slice_bitcast_fusion.21), kind=kOutput, calls=%fused_computation.5.clone.1 | convolution fusion | flops 405798912 | bytes 3162112 | tf_op jit(solution)/shard_map/while/body/tcrp,tpq->tcrq/dot_general | solution.py:41
  227.6 10.6 %fusion.102 = f32[8,2,32,256]{3,2,1,0:T(8,128)S(1)} fusion(f32[8,2,32,256]{3,2,1,0:T(8,128)S(1)} %get-tuple-element.291, f32[8,256,256]{2,1,0:T(8,128)S(1)} %multiply_reduce_fusion.2, f32[8,256]{1,0:T(8,128)S(1)} %slice_bitcast_fusion.20, f32[8,256]{1,0:T(8,128)S(1)} %slice_bitcast_fusion.21), kind=kOutput, calls=%fused_computation.1.clone.1 | convolution fusion | flops 405798912 | bytes 3162112 | tf_op jit(solution)/shard_map/while/body/tcrp,tpq->tcrq/dot_general | solution.py:44
  238.2 10.8 %fusion.101 = f32[8,2,32,256]{3,2,1,0:T(8,128)S(1)} fusion(f32[8,2,32,256]{3,2,1,0:T(8,128)S(1)} %get-tuple-element.270, f32[8,256,256]{2,1,0:T(8,128)S(1)} %multiply_reduce_fusion.2, f32[8,256]{1,0:T(8,128)S(1)} %slice_bitcast_fusion.20, f32[8,256]{1,0:T(8,128)S(1)} %slice_bitcast_fusion.21), kind=kOutput, calls=%fused_computation.7.clone.1 | convolution fusion | flops 405798912 | bytes 3162112 | tf_op jit(solution)/shard_map/while/body/tcrq,tpq->tcrp/dot_general | solution.py:41
  249.1 10.9 %fusion.100 = f32[8,2,32,256]{3,2,1,0:T(8,128)S(1)} fusion(f32[8,2,32,256]{3,2,1,0:T(8,128)S(1)} %get-tuple-element.270, f32[8,256,256]{2,1,0:T(8,128)S(1)} %multiply_reduce_fusion.2, f32[8,256]{1,0:T(8,128)S(1)} %slice_bitcast_fusion.20, f32[8,256]{1,0:T(8,128)S(1)} %slice_bitcast_fusion.21), kind=kOutput, calls=%fused_computation.3.clone.1 | convolution fusion | flops 405798912 | bytes 3162112 | tf_op jit(solution)/shard_map/while/body/tcrq,tpq->tcrp/dot_general | solution.py:44
  278.7 0.9 bitcast_dynamic-update-slice_fusion.31
  279.7 1.1 multiply_reduce_fusion.2
  280.8 10.4 %fusion.103 = f32[8,2,32,256]{3,2,1,0:T(8,128)S(1)} fusion(f32[8,2,32,256]{3,2,1,0:T(8,128)S(1)} %get-tuple-element.291, f32[8,256,256]{2,1,0:T(8,128)S(1)} %multiply_reduce_fusion.2, f32[8,256]{1,0:T(8,128)S(1)} %slice_bitcast_fusion.20, f32[8,256]{1,0:T(8,128)S(1)} %slice_bitcast_fusion.21), kind=kOutput, calls=%fused_computation.5.clone.1 | convolution fusion | flops 405798912 | bytes 3162112 | tf_op jit(solution)/shard_map/while/body/tcrp,tpq->tcrq/dot_general | solution.py:41
  291.2 10.6 %fusion.102 = f32[8,2,32,256]{3,2,1,0:T(8,128)S(1)} fusion(f32[8,2,32,256]{3,2,1,0:T(8,128)S(1)} %get-tuple-element.291, f32[8,256,256]{2,1,0:T(8,128)S(1)} %multiply_reduce_fusion.2, f32[8,256]{1,0:T(8,128)S(1)} %slice_bitcast_fusion.20, f32[8,256]{1,0:T(8,128)S(1)} %slice_bitcast_fusion.21), kind=kOutput, calls=%fused_computation.1.clone.1 | convolution fusion | flops 405798912 | bytes 3162112 | tf_op jit(solution)/shard_map/while/body/tcrp,tpq->tcrq/dot_general | solution.py:44
  301.9 10.8 %fusion.101 = f32[8,2,32,256]{3,2,1,0:T(8,128)S(1)} fusion(f32[8,2,32,256]{3,2,1,0:T(8,128)S(1)} %get-tuple-element.270, f32[8,256,256]{2,1,0:T(8,128)S(1)} %multiply_reduce_fusion.2, f32[8,256]{1,0:T(8,128)S(1)} %slice_bitcast_fusion.20, f32[8,256]{1,0:T(8,128)S(1)} %slice_bitcast_fusion.21), kind=kOutput, calls=%fused_computation.7.clone.1 | convolution fusion | flops 405798912 | bytes 3162112 | tf_op jit(solution)/shard_map/while/body/tcrq,tpq->tcrp/dot_general | solution.py:41
  312.8 10.9 %fusion.100 = f32[8,2,32,256]{3,2,1,0:T(8,128)S(1)} fusion(f32[8,2,32,256]{3,2,1,0:T(8,128)S(1)} %get-tuple-element.270, f32[8,256,256]{2,1,0:T(8,128)S(1)} %multiply_reduce_fusion.2, f32[8,256]{1,0:T(8,128)S(1)} %slice_bitcast_fusion.20, f32[8,256]{1,0:T(8,128)S(1)} %slice_bitcast_fusion.21), kind=kOutput, calls=%fused_computation.3.clone.1 | convolution fusion | flops 405798912 | bytes 3162112 | tf_op jit(solution)/shard_map/while/body/tcrq,tpq->tcrp/dot_general | solution.py:44
  343.3 1.1 multiply_reduce_fusion.2
  344.4 10.4 %fusion.103 = f32[8,2,32,256]{3,2,1,0:T(8,128)S(1)} fusion(f32[8,2,32,256]{3,2,1,0:T(8,128)S(1)} %get-tuple-element.291, f32[8,256,256]{2,1,0:T(8,128)S(1)} %multiply_reduce_fusion.2, f32[8,256]{1,0:T(8,128)S(1)} %slice_bitcast_fusion.20, f32[8,256]{1,0:T(8,128)S(1)} %slice_bitcast_fusion.21), kind=kOutput, calls=%fused_computation.5.clone.1 | convolution fusion | flops 405798912 | bytes 3162112 | tf_op jit(solution)/shard_map/while/body/tcrp,tpq->tcrq/dot_general | solution.py:41
  354.9 10.6 %fusion.102 = f32[8,2,32,256]{3,2,1,0:T(8,128)S(1)} fusion(f32[8,2,32,256]{3,2,1,0:T(8,128)S(1)} %get-tuple-element.291, f32[8,256,256]{2,1,0:T(8,128)S(1)} %multiply_reduce_fusion.2, f32[8,256]{1,0:T(8,128)S(1)} %slice_bitcast_fusion.20, f32[8,256]{1,0:T(8,128)S(1)} %slice_bitcast_fusion.21), kind=kOutput, calls=%fused_computation.1.clone.1 | convolution fusion | flops 405798912 | bytes 3162112 | tf_op jit(solution)/shard_map/while/body/tcrp,tpq->tcrq/dot_general | solution.py:44
  365.5 10.8 %fusion.101 = f32[8,2,32,256]{3,2,1,0:T(8,128)S(1)} fusion(f32[8,2,32,256]{3,2,1,0:T(8,128)S(1)} %get-tuple-element.270, f32[8,256,256]{2,1,0:T(8,128)S(1)} %multiply_reduce_fusion.2, f32[8,256]{1,0:T(8,128)S(1)} %slice_bitcast_fusion.20, f32[8,256]{1,0:T(8,128)S(1)} %slice_bitcast_fusion.21), kind=kOutput, calls=%fused_computation.7.clone.1 | convolution fusion | flops 405798912 | bytes 3162112 | tf_op jit(solution)/shard_map/while/body/tcrq,tpq->tcrp/dot_general | solution.py:41
  376.4 10.9 %fusion.100 = f32[8,2,32,256]{3,2,1,0:T(8,128)S(1)} fusion(f32[8,2,32,256]{3,2,1,0:T(8,128)S(1)} %get-tuple-element.270, f32[8,256,256]{2,1,0:T(8,128)S(1)} %multiply_reduce_fusion.2, f32[8,256]{1,0:T(8,128)S(1)} %slice_bitcast_fusion.20, f32[8,256]{1,0:T(8,128)S(1)} %slice_bitcast_fusion.21), kind=kOutput, calls=%fused_computation.3.clone.1 | convolution fusion | flops 405798912 | bytes 3162112 | tf_op jit(solution)/shard_map/while/body/tcrq,tpq->tcrp/dot_general | solution.py:44
  403.4 0.9 bitcast_dynamic-update-slice_fusion.28
  405.2 0.9 bitcast_dynamic-update-slice_fusion.30
  407.1 1.1 multiply_reduce_fusion.2
  408.2 10.4 %fusion.103 = f32[8,2,32,256]{3,2,1,0:T(8,128)S(1)} fusion(f32[8,2,32,256]{3,2,1,0:T(8,128)S(1)} %get-tuple-element.291, f32[8,256,256]{2,1,0:T(8,128)S(1)} %multiply_reduce_fusion.2, f32[8,256]{1,0:T(8,128)S(1)} %slice_bitcast_fusion.20, f32[8,256]{1,0:T(8,128)S(1)} %slice_bitcast_fusion.21), kind=kOutput, calls=%fused_computation.5.clone.1 | convolution fusion | flops 405798912 | bytes 3162112 | tf_op jit(solution)/shard_map/while/body/tcrp,tpq->tcrq/dot_general | solution.py:41
  418.7 10.6 %fusion.102 = f32[8,2,32,256]{3,2,1,0:T(8,128)S(1)} fusion(f32[8,2,32,256]{3,2,1,0:T(8,128)S(1)} %get-tuple-element.291, f32[8,256,256]{2,1,0:T(8,128)S(1)} %multiply_reduce_fusion.2, f32[8,256]{1,0:T(8,128)S(1)} %slice_bitcast_fusion.20, f32[8,256]{1,0:T(8,128)S(1)} %slice_bitcast_fusion.21), kind=kOutput, calls=%fused_computation.1.clone.1 | convolution fusion | flops 405798912 | bytes 3162112 | tf_op jit(solution)/shard_map/while/body/tcrp,tpq->tcrq/dot_general | solution.py:44
  429.3 10.8 %fusion.101 = f32[8,2,32,256]{3,2,1,0:T(8,128)S(1)} fusion(f32[8,2,32,256]{3,2,1,0:T(8,128)S(1)} %get-tuple-element.270, f32[8,256,256]{2,1,0:T(8,128)S(1)} %multiply_reduce_fusion.2, f32[8,256]{1,0:T(8,128)S(1)} %slice_bitcast_fusion.20, f32[8,256]{1,0:T(8,128)S(1)} %slice_bitcast_fusion.21), kind=kOutput, calls=%fused_computation.7.clone.1 | convolution fusion | flops 405798912 | bytes 3162112 | tf_op jit(solution)/shard_map/while/body/tcrq,tpq->tcrp/dot_general | solution.py:41
  440.2 10.9 %fusion.100 = f32[8,2,32,256]{3,2,1,0:T(8,128)S(1)} fusion(f32[8,2,32,256]{3,2,1,0:T(8,128)S(1)} %get-tuple-element.270, f32[8,256,256]{2,1,0:T(8,128)S(1)} %multiply_reduce_fusion.2, f32[8,256]{1,0:T(8,128)S(1)} %slice_bitcast_fusion.20, f32[8,256]{1,0:T(8,128)S(1)} %slice_bitcast_fusion.21), kind=kOutput, calls=%fused_computation.3.clone.1 | convolution fusion | flops 405798912 | bytes 3162112 | tf_op jit(solution)/shard_map/while/body/tcrq,tpq->tcrp/dot_general | solution.py:44
  451.9 4.5 collective-permute-start.2
  456.4 19.8 %collective-permute-done.2 = f32[2,32,4096]{2,1,0:T(8,128)S(1)} collective-permute-done((f32[2,32,4096]{2,1,0:T(8,128)S(1)}, f32[2,32,4096]{2,1,0:T(8,128)S(1)}, u32[]{:S(2)}, u32[]{:S(2)}) %collective-permute-start.2) | collective-permute-done | bytes 1048608 | tf_op jit(solution)/shard_map/ppermute | solution.py:22
  476.1 1.1 slice_add_fusion.2
  477.3 93.9 %reduce-scatter.2.cloned.1.call-done = f32[2,32,512]{2,1,0:T(8,128)} async-done(((f32[2,32,4096]{2,1,0:T(8,128)}), f32[2,32,512]{2,1,0:T(8,128)}) %reduce-scatter.2.cloned.1.call-update) | async-done | bytes 131088 | tf_op jit(solution)/shard_map/reduce_scatter | solution.py:148
  (351 shorter events, 57.4 us)
Async XLA Ops:
  6.5 33.9 %all-gather.2.cloned.1.call-start = ((), (), s32[]{:S(2)}) async-start(), calls=%async_computation.1 | async-start | bytes 1179648 | tf_op jit(solution)/shard_map/all_gather | solution.py:69
  7.3 563.9 %reduce-scatter.2.cloned.1.call-start = ((), (), s32[]{:S(2)}) async-start(), calls=%async_computation.2 | async-start | bytes 1179648 | tf_op jit(solution)/shard_map/reduce_scatter | solution.py:148
  28.6 14.1 %collective-permute-start.1 = (f32[4,4096]{1,0:T(4,128)S(1)}, f32[4,4096]{1,0:T(4,128)S(1)}, u32[]{:S(2)}, u32[]{:S(2)}) collective-permute-start(f32[4,4096]{1,0:T(4,128)S(1)} %all_gather.15), channel_id=1, source_target_pairs={{8,0},{16,8},{24,16},{9,1},{17,9},{25,17},{10,2},{18,10},{26,18},{... | collective-permute-start | bytes 196616 | tf_op jit(solution)/shard_map/ppermute | solution.py:22
  40.4 26.4 %collective-permute-start = (f32[2,32,4096]{2,1,0:T(8,128)}, f32[2,32,4096]{2,1,0:T(8,128)S(1)}, u32[]{:S(2)}, u32[]{:S(2)}) collective-permute-start(f32[2,32,4096]{2,1,0:T(8,128)} %all-gather.2.cloned.1.call-done), channel_id=1, source_target_pairs={{8,0},{16,8},{24,16},{9,1},{17,9},{25,17},{10,2},{18,10},{26,18},{... | collective-permute-start | bytes 3145736 | tf_op jit(solution)/shard_map/ppermute | solution.py:22
  451.9 24.3 %collective-permute-start.2 = (f32[2,32,4096]{2,1,0:T(8,128)S(1)}, f32[2,32,4096]{2,1,0:T(8,128)S(1)}, u32[]{:S(2)}, u32[]{:S(2)}) collective-permute-start(f32[2,32,4096]{2,1,0:T(8,128)S(1)} %slice.180), channel_id=1, source_target_pairs={{0,8},{8,16},{16,24},{1,9},{9,17},{17,25},{2,10},{10,18},{18,26},{... | collective-permute-start | bytes 3145736 | tf_op jit(solution)/shard_map/ppermute | solution.py:22
Sparse Core Ops, SparseCore 0:
  9.0 24.8 all-gather.1
  477.4 93.7 reduce-scatter.1
where the time goes:
time: 581 us; the launch traced here: 578 us
  matrix products  257 us (44%)
  waiting for transfers between devices  138 us (24%)
  loops' own time  61.4 us (11%)
  local copies, waits for them, and re-layouts  56.5 us (10%)
  blocking collectives  24.8 us (4%)
  other arithmetic  17.4 us (3%)
  between operations  15.5 us (3%)
  starting transfers between devices  7.08 us (1%)
    dot_general x12, matrix products, batch_apply(): jnp.einsum(form, vectors, imag_part, precision=highest, preferred_element...  129 us
    dot_general x12, matrix products, batch_apply(): jnp.einsum(form, vectors, real_part, precision=highest, preferred_element...  128 us
    reduce_scatter x1, waiting for transfers between devices, body(): lax.psum_scatter(own_part + carried, 'dev', scatter_dimension=2, tiled=True)  93.9 us
    another operation x1, loops' own time, body(): accumulated = lax.fori_loop(0, turns, one_turn, accumulated)  61.4 us
    ppermute x3, waiting for transfers between devices, from_behind(): lax.ppermute(value, axis, [(source, source + steps) for source in range(i...  43.8 us
    while x42, local copies, waits for them, and re-layouts  37.8 us
    all_gather x1, blocking collectives, body(): lax.all_gather(geometry, 'dev', axis=1, tiled=True)  15.6 us
  transfers between devices with their start and end apart: 5, of which 3 were waited for; matrix products, arithmetic and copies ran while one was open for 1% of the time, Pallas kernels for 0%

commit v1 on v0

v1 whole, which is shorter than its diff:
```python
import functools
import math

import jax
import jax.numpy as jnp
from jax import lax
from jax.experimental import pallas as pl
from jax.experimental.pallas import tpu as pltpu
from jax.sharding import PartitionSpec as P

BLOCK = 256
STRIP = 16
VMEM_LIMIT = 48 * 1024 * 1024

wave_number = 25.0
smoothing = 0.05
per_unit = wave_number / (2.0 * math.pi)
core_sq = (smoothing * per_unit) ** 2
amplitude = per_unit / (4.0 * math.pi)
SINE = (4.4428679, -7.30744342, 3.59478806, -0.78437397)
COSINE = (1.4142135, -6.97885099, 5.73946117, -1.88356297, 0.31069815)

COUNT_ROW = 3
WEIGHT_ROW = 4
EXTRA = 8


def horner(z, terms):
    value = z * terms[-1] + terms[-2]
    for term in terms[-3::-1]:
        value = value * z + term
    return value


def wave(near, far):
    square = None
    for a, b in zip(near, far):
        gap = a - b
        gap = gap * gap
        square = gap + core_sq if square is None else square + gap
    inverse = lax.rsqrt(square)
    turns = square * inverse
    part = turns - jnp.round(turns)
    z = part * part
    s = horner(z, SINE) * part
    scaled = inverse * s
    return inverse - scaled * s, scaled * horner(z, COSINE)


def pack_kernel(width, drive, coords, rules, rule_weight, pair_cols, pair_count, out):
    patterns = drive.shape[1]
    first_row = (lax.axis_index("band") * lax.axis_size("dev") + lax.axis_index("dev")) * 2
    weight = jnp.zeros(rules.shape, jnp.float32)
    for rule in range(rule_weight.shape[0]):
        weight = jnp.where(rules[...] == rule, rule_weight[rule], weight)
    scale = weight * amplitude
    out[0:patterns, :] = drive[0] * scale
    out[patterns : 2 * patterns, :] = drive[1] * scale
    lanes = lax.broadcasted_iota(jnp.int32, rules.shape, 1)

    def count(slot, totals):
        odd = lax.rem(slot, 2)
        place = pair_cols[slot] - first_row - odd + odd * width
        return totals + jnp.where(lanes == place, 1.0, 0.0)

    counts = lax.fori_loop(0, pair_count[0], count, jnp.zeros(rules.shape, jnp.float32))
    base = 2 * patterns
    out[base : base + EXTRA, :] = jnp.zeros((EXTRA, out.shape[1]), jnp.float32)
    out[base : base + 3, :] = coords[...] * per_unit
    out[base + COUNT_ROW : base + COUNT_ROW + 1, :] = counts
    out[base + WEIGHT_ROW : base + WEIGHT_ROW + 1, :] = weight


def near_kernel(groups, first_block, blocks, width, has_start, *refs):
    cols = refs[:blocks]
    points = refs[blocks : blocks + 3]
    refs = refs[blocks + 3 :]
    start, refs = (refs[0], refs[1:]) if has_start else (None, refs)
    out, left, across, row_points, hi_a, lo_a, hi_b, lo_b, acc, tables, plan, factor, sem = refs
    base = cols[0].shape[0] - EXTRA
    half = base // 2
    lanes = tables.shape[2]
    n_rows = 2 * len(groups)
    copies = [
        pltpu.make_async_copy(
            cols[s].at[base : base + EXTRA, 0:lanes], tables.at[s], sem.at[s]
        )
        for s in range(blocks)
    ] + [
        pltpu.make_async_copy(
            points[g].at[:, 0:lanes], tables.at[blocks + g], sem.at[blocks + g]
        )
        for g in range(2)
    ]
    for copy in copies:
        copy.start()
    for s in range(blocks):
        for h in range(2):
            span = slice(h * BLOCK, (h + 1) * BLOCK)
            x = cols[s][0:base, span]
            wide = jnp.concatenate([x, jnp.concatenate([-x[half:], x[:half]], 0)], 1)
            hi = wide.astype(jnp.bfloat16)
            left[2 * s + h, 0:base, :] = hi
            left[2 * s + h, base : 2 * base, :] = (wide - hi.astype(jnp.float32)).astype(
                jnp.bfloat16
            )
            across[2 * s + h, :, 0:EXTRA] = cols[s][base : base + EXTRA, span].T
    for k, g in enumerate(groups):
        for r in range(2):
            row_points[2 * k + r] = points[g + 1][:, r * BLOCK : (r + 1) * BLOCK]
            if has_start:
                acc[2 * k + r] = start[k, :, r * BLOCK : (r + 1) * BLOCK]
            else:
                acc[2 * k + r] = jnp.zeros(acc.shape[1:], jnp.float32)
    for copy in copies:
        copy.wait()

    me = lax.axis_index("dev")

    def add_column(col, total):
        s = col // 2
        h = lax.rem(col, 2)
        place = 2 * jnp.bitwise_xor(me, s + first_block) + h
        for k, g in enumerate(groups):
            for r in range(2):
                gap = g * width + 2 * me + r - place
                ahead = tables[s, COUNT_ROW, h * width + jnp.clip(gap, 0, width - 1)]
                value = jnp.where((gap >= 0) & (gap < width), ahead, 0.0)
                if g < 1:
                    behind = tables[
                        blocks + 1 + g, COUNT_ROW, r * width + jnp.clip(-gap, 0, width - 1)
                    ]
                    value = jnp.where((gap < 0) & (gap > -width), behind, value)
                plan[total] = col * n_rows + 2 * k + r
                factor[total] = value
                total = total + jnp.where(value > 0.0, 1, 0)
        return total

    live = lax.fori_loop(0, 2 * blocks, add_column, jnp.int32(0))
    for k in range(2):
        plan[live + k] = 0
        factor[live + k] = 0.0

    def build(tile, hi_ref, lo_ref):
        entry = plan[tile]
        col = entry // n_rows
        row = lax.rem(entry, n_rows)
        far = [row_points[row, k : k + 1, :] for k in range(3)]
        for at in range(0, BLOCK, STRIP):
            near = [across[col, at : at + STRIP, k : k + 1] for k in range(3)]
            for part, first in zip(wave(near, far), (0, BLOCK)):
                hi = part.astype(jnp.bfloat16)
                hi_ref[first + at : first + at + STRIP, :] = hi
                lo_ref[first + at : first + at + STRIP, :] = (
                    part - hi.astype(jnp.float32)
                ).astype(jnp.bfloat16)

    def apply(tile, hi_ref, lo_ref):
        entry = plan[tile]
        col = entry // n_rows
        row = lax.rem(entry, n_rows)
        top = jnp.dot(left[col], hi_ref[...], preferred_element_type=jnp.float32)
        rest = jnp.dot(left[col, 0:base], lo_ref[...], preferred_element_type=jnp.float32)
        acc[row] += factor[tile] * (top[:base] + top[base:] + rest)

    @pl.when(live > 0)
    def _():
        build(0, hi_a, lo_a)

        def pair(i, carry):
            apply(2 * i, hi_a, lo_a)
            build(2 * i + 1, hi_b, lo_b)
            apply(2 * i + 1, hi_b, lo_b)
            build(2 * i + 2, hi_a, lo_a)
            return carry

        lax.fori_loop(0, (live + 1) // 2, pair, 0)

    for k in range(len(groups)):
        for r in range(2):
            out[k, :, r * BLOCK : (r + 1) * BLOCK] = acc[2 * k + r]


def near_part(groups, first_block, cols, points, width, start=None):
    blocks = len(cols)
    rows, own = cols[0].shape
    base = rows - EXTRA
    lanes = -(-2 * width // 128) * 128
    n_rows = 2 * len(groups)
    kernel = functools.partial(
        near_kernel, groups, first_block, blocks, width, start is not None
    )
    args = list(cols) + list(points) + ([] if start is None else [start])
    tile = pltpu.VMEM((2 * BLOCK, BLOCK), jnp.bfloat16)
    tiles = blocks * 2 * n_rows
    return pl.pallas_call(
        kernel,
        out_shape=jax.ShapeDtypeStruct((len(groups), base, own), jnp.float32),
        in_specs=[pl.BlockSpec(memory_space=pltpu.VMEM)] * len(args),
        out_specs=pl.BlockSpec(memory_space=pltpu.VMEM),
        scratch_shapes=[
            pltpu.VMEM((2 * blocks, 2 * base, 2 * BLOCK), jnp.bfloat16),
            pltpu.VMEM((2 * blocks, BLOCK, 128), jnp.float32),
            pltpu.VMEM((n_rows, EXTRA, BLOCK), jnp.float32),
            tile,
            tile,
            tile,
            tile,
            pltpu.VMEM((n_rows, base, BLOCK), jnp.float32),
            pltpu.SMEM((blocks + 2, EXTRA, lanes), jnp.float32),
            pltpu.SMEM((tiles + 8,), jnp.int32),
            pltpu.SMEM((tiles + 8,), jnp.float32),
            pltpu.SemaphoreType.DMA((blocks + 2,)),
        ],
        compiler_params=pltpu.CompilerParams(vmem_limit_bytes=VMEM_LIMIT),
        cost_estimate=pl.CostEstimate(
            flops=tiles * 6 * 4 * base * BLOCK * BLOCK // 2,
            bytes_accessed=4 * rows * own * (blocks + 3),
            transcendentals=tiles * BLOCK * BLOCK,
        ),
    )(*args)


def shifted(value, axis, steps):
    count = lax.axis_size(axis)
    first, last = max(0, -steps), min(count, count - steps)
    return lax.ppermute(value, axis, [(i, i + steps) for i in range(first, last)])


def swapped(value, axis, mask):
    return lax.ppermute(value, axis, [(i, i ^ mask) for i in range(lax.axis_size(axis))])


def body(drive, coords, rule_index, rule_weight, pair_cols, pair_count):
    n_dev = lax.axis_size("dev")
    patterns, own = drive.shape[1:]
    width = n_dev * (own // BLOCK)
    vmem, smem = (pl.BlockSpec(memory_space=m) for m in (pltpu.VMEM, pltpu.SMEM))
    payload = pl.pallas_call(
        functools.partial(pack_kernel, width),
        out_shape=jax.ShapeDtypeStruct((2 * patterns + EXTRA, own), jnp.float32),
        in_specs=[vmem, vmem, vmem, smem, smem, smem],
        out_specs=vmem,
    )(drive, coords, rule_index[None, :], rule_weight, pair_cols, pair_count)
    base = 2 * patterns
    mine = payload[base:]
    points = (shifted(mine, "band", 1), mine, shifted(mine, "band", -1))
    same = {0: payload}
    for mask in range(2, n_dev, 2):
        same[mask] = swapped(payload, "dev", mask)
    held = dict(same)
    for mask, value in same.items():
        held[mask + 1] = swapped(value, "dev", 1)
    first = near_part((-1, 0, 1), 0, [held[0], held[1]], points, width)
    later = [held[mask] for mask in range(2, n_dev)]
    edges = near_part((-1, 1), 2, later, points, width, first[0::2])
    from_after = shifted(edges[0], "band", -1)
    from_before = shifted(edges[1], "band", 1)
    middle = near_part((0,), 2, later, points, width, first[1:2])
    total = (middle[0] + from_after + from_before) * mine[WEIGHT_ROW]
    return total.reshape(drive.shape)


def solution(mesh):
    spread = ("band", "dev")
    in_specs = (
        P(None, None, spread),
        P(None, spread),
        P(spread),
        P(),
        P(spread),
        P(spread),
    )
    out_specs = P(None, None, spread)
    return jax.shard_map(body, mesh=mesh, in_specs=in_specs, out_specs=out_specs, check_vma=False)
```

time: 581 us -> 67.6 us (0.12)
  matrix products: 257 us -> 0 us
  waiting for transfers between devices: 138 us -> 18 us
  loops' own time: 61.4 us -> 0 us
  local copies, waits for them, and re-layouts: 56.5 us -> 2.4 us
  Pallas kernels: 0 us -> 26.1 us
  blocking collectives: 24.8 us -> 0 us
  other arithmetic: 17.4 us -> 0.69 us
  between operations: 15.5 us -> 0.78 us
  starting transfers between devices: 7.08 us -> 18.5 us
    dot_general x24 -> x0, matrix products: 257 us -> none  [the longest x12 129 us: batch_apply(): jnp.einsum(form, vectors, imag_part, precision=highest, preferred_element...]
    reduce_scatter x1 -> x0, waiting for transfers between devices: 93.9 us -> none  [body(): lax.psum_scatter(own_part + carried, 'dev', scatter_dimension=2, tiled=True)]
    another operation x1 -> x0, loops' own time: 61.4 us -> none  [body(): accumulated = lax.fori_loop(0, turns, one_turn, accumulated)]
    while x42 -> x0, local copies, waits for them, and re-layouts: 37.8 us -> none
    pallas_call x0 -> x4, Pallas kernels: none -> 26.1 us  [the longest x3 24.1 us: near_part(): pl.pallas_call(kernel, out_shape=jax.ShapeDtypeStruct((len(groups), base,...]
    ppermute x3 -> x11, waiting for transfers between devices: 43.8 us -> 18 us  [the longest x7 12.3 us: swapped(): lax.ppermute(value, axis, [(i, i ^ mask) for i in range(lax.axis_size(axi...]
    all_gather x1 -> x0, blocking collectives: 15.6 us -> none  [body(): lax.all_gather(geometry, 'dev', axis=1, tiled=True)]
    ppermute x3 -> x11, starting transfers between devices: 7.04 us -> 18.5 us  [the longest x4 12.4 us: shifted(): lax.ppermute(value, axis, [(i, i + steps) for i in range(first, last)])]
  transfers between devices with their start and end apart: 5 -> 11, of which waited for: 3 -> 4; matrix products, arithmetic and copies ran while one was open for 1% -> 2% of each run, Pallas kernels for 0% -> 22%
where the time goes in v1:
time: 67.6 us; the launch traced here: 66.5 us
  Pallas kernels  26.1 us (39%)
  starting transfers between devices  18.5 us (27%)
  waiting for transfers between devices  18 us (27%)
  local copies, waits for them, and re-layouts  2.4 us (4%)
  between operations  0.78 us (1%)
  other arithmetic  0.69 us (1%)
    pallas_call x3, Pallas kernels, near_part(): pl.pallas_call(kernel, out_shape=jax.ShapeDtypeStruct((len(groups), base,...  24.1 us
    ppermute x4, starting transfers between devices, shifted(): lax.ppermute(value, axis, [(i, i + steps) for i in range(first, last)])  12.4 us
    ppermute x7, waiting for transfers between devices, swapped(): lax.ppermute(value, axis, [(i, i ^ mask) for i in range(lax.axis_size(axi...  12.3 us
    ppermute x7, starting transfers between devices, swapped(): lax.ppermute(value, axis, [(i, i ^ mask) for i in range(lax.axis_size(axi...  6.1 us
    ppermute x4, waiting for transfers between devices, shifted(): lax.ppermute(value, axis, [(i, i + steps) for i in range(first, last)])  5.76 us
    pallas_call x1, Pallas kernels, body(): pl.pallas_call(functools.partial(pack_kernel, width), out_shape=jax.Shape...  1.98 us
  transfers between devices with their start and end apart: 11, of which 4 were waited for; matrix products, arithmetic and copies ran while one was open for 2% of the time, Pallas kernels for 22%

profile of v1, /device:TPU:0, one launch (start us, length us, event | category | flops | bytes accessed | tf_op | source)
XLA Modules:
  0.0 66.5 jit_solution(16838222618954973589)
XLA Ops:
  0.7 2.0 %shard_map.64.refs_0_ = f32[72,512]{1,0:T(8,128)} custom-call(f32[2,32,512]{2,1,0:T(8,128)} %drive.1, f32[3,512]{1,0:T(4,128)} %coords.1, s32[1,512]{1,0:T(1,128)} %bitcast.14, f32[4]{0:T(128)} %rule_weight.1, s32[96]{0:T(128)} %pair_cols.1, s32[1]{0:T(128)S(6)} %copy.7.pair_count), custom_call_target="tpu_custom_call" | custom-call | tf_op jit(solution)/shard_map/pallas_call | solution.py:239
  2.6 5.0 %collective-permute-start.4 = (f32[72,512]{1,0:T(8,128)}, f32[72,512]{1,0:T(8,128)S(1)}, u32[]{:S(2)}, u32[]{:S(2)}) collective-permute-start(f32[72,512]{1,0:T(8,128)} %shard_map.64.refs_0_), channel_id=1, source_target_pairs={{0,6},{1,7},{2,4},{3,5},{4,2},{5,3},{6,0},{7,1},{8,14},{9,15},{10,... | collective-permute-start | bytes 442376 | tf_op jit(solution)/shard_map/ppermute | solution.py:231
  7.7 0.0 collective-permute-start.2
  7.7 0.6 collective-permute-start
  8.2 0.0 collective-permute-start.8
  8.2 4.4 %collective-permute-done.4.refs_4_ = f32[72,512]{1,0:T(8,128)S(1)} collective-permute-done((f32[72,512]{1,0:T(8,128)}, f32[72,512]{1,0:T(8,128)S(1)}, u32[]{:S(2)}, u32[]{:S(2)}) %collective-permute-start.4) | collective-permute-done | bytes 147488 | tf_op jit(solution)/shard_map/ppermute | solution.py:231
  12.6 0.0 collective-permute-start.5
  12.6 7.8 %collective-permute-done.2.refs_2_ = f32[72,512]{1,0:T(8,128)S(1)} collective-permute-done((f32[72,512]{1,0:T(8,128)}, f32[72,512]{1,0:T(8,128)S(1)}, u32[]{:S(2)}, u32[]{:S(2)}) %collective-permute-start.2) | collective-permute-done | bytes 147488 | tf_op jit(solution)/shard_map/ppermute | solution.py:231
  20.5 0.0 collective-permute-start.3
  20.5 0.0 collective-permute-done.refs_0_
  20.5 0.5 collective-permute-start.1
  21.0 0.7 %slice.25.refs_3_.refs_7_ = f32[8,512]{1,0:T(8,128)S(1)} slice(f32[72,512]{1,0:T(8,128)} %shard_map.64.refs_0_), slice={[64:72], [0:512]} | slice | bytes 32768 | tf_op jit(solution)/shard_map/slice | solution.py:246
  21.7 1.3 %collective-permute-start.7 = (f32[8,512]{1,0:T(8,128)S(1)}, f32[8,512]{1,0:T(8,128)S(1)}, u32[]{:S(2)}, u32[]{:S(2)}) collective-permute-start(f32[8,512]{1,0:T(8,128)S(1)} %slice.25.refs_3_.refs_7_), channel_id=1, source_target_pairs={{8,0},{16,8},{24,16},{9,1},{17,9},{25,17},{10,2},{18,10},{26,18},{... | collective-permute-start | bytes 49160 | tf_op jit(solution)/shard_map/ppermute | solution.py:227
  23.0 4.3 %collective-permute-done.7.refs_4_.refs_8_ = f32[8,512]{1,0:T(8,128)S(1)} collective-permute-done((f32[8,512]{1,0:T(8,128)S(1)}, f32[8,512]{1,0:T(8,128)S(1)}, u32[]{:S(2)}, u32[]{:S(2)}) %collective-permute-start.7) | collective-permute-done | bytes 16416 | tf_op jit(solution)/shard_map/ppermute | solution.py:227
  27.3 4.2 %collective-permute-start.6 = (f32[8,512]{1,0:T(8,128)S(1)}, f32[8,512]{1,0:T(8,128)S(1)}, u32[]{:S(2)}, u32[]{:S(2)}) collective-permute-start(f32[8,512]{1,0:T(8,128)S(1)} %slice.25.refs_3_.refs_7_), channel_id=1, source_target_pairs={{0,8},{8,16},{16,24},{1,9},{9,17},{17,25},{2,10},{10,18},{18,26},{... | collective-permute-start | bytes 49160 | tf_op jit(solution)/shard_map/ppermute | solution.py:227
  31.6 1.4 %collective-permute-done.6.refs_2_.refs_6_ = f32[8,512]{1,0:T(8,128)S(1)} collective-permute-done((f32[8,512]{1,0:T(8,128)S(1)}, f32[8,512]{1,0:T(8,128)S(1)}, u32[]{:S(2)}, u32[]{:S(2)}) %collective-permute-start.6) | collective-permute-done | bytes 16416 | tf_op jit(solution)/shard_map/ppermute | solution.py:227
  33.0 0.0 collective-permute-done.8.refs_1_
  33.0 0.0 copy-start
  33.0 0.9 %copy-done = f32[72,512]{1,0:T(8,128)S(1)} copy-done((f32[72,512]{1,0:T(8,128)S(1)}, f32[72,512]{1,0:T(8,128)}, u32[]{:S(2)}) %copy-start) | copy-done | bytes 147480
  33.9 5.6 %shard_map.65 = f32[3,64,512]{2,1,0:T(8,128)S(1)} custom-call(f32[72,512]{1,0:T(8,128)S(1)} %copy-done, f32[72,512]{1,0:T(8,128)S(1)} %collective-permute-done.8.refs_1_, f32[8,512]{1,0:T(8,128)S(1)} %collective-permute-done.6.refs_2_.refs_6_, f32[8,512]{1,0:T(8,128)S(1)} %slice.25.refs_3_.refs_7_, f32[8,512]{1,0:T(8,128)S(1)} %collective-permute-done.7.refs_4_.refs_8_), custom_call_target="tpu_custom_call" | custom-call | flops 1207959552 | bytes 737280 | tf_op jit(solution)/shard_map/pallas_call | solution.py:196
  39.5 0.0 collective-permute-done.5.refs_5_
  39.5 0.0 collective-permute-done.3.refs_3_
  39.5 0.0 collective-permute-done.1.refs_1_
  39.6 9.4 %shard_map.67 = f32[2,64,512]{2,1,0:T(8,128)S(1)} custom-call(f32[72,512]{1,0:T(8,128)S(1)} %collective-permute-done.refs_0_, f32[72,512]{1,0:T(8,128)S(1)} %collective-permute-done.1.refs_1_, f32[72,512]{1,0:T(8,128)S(1)} %collective-permute-done.2.refs_2_, f32[72,512]{1,0:T(8,128)S(1)} %collective-permute-done.3.refs_3_, ...), custom_call_target="tpu_custom_call" | custom-call | flops 2415919104 | bytes 1327104 | tf_op jit(solution)/shard_map/pallas_call | solution.py:196
  49.0 1.3 %collective-permute-start.9 = (f32[64,512]{1,0:T(8,128)S(1)}, f32[64,512]{1,0:T(8,128)S(1)}, u32[]{:S(2)}, u32[]{:S(2)}) collective-permute-start(f32[64,512]{1,0:T(8,128)S(1)} %get-tuple-element.5), channel_id=1, source_target_pairs={{8,0},{16,8},{24,16},{9,1},{17,9},{25,17},{10,2},{18,10},{26,18},{... | collective-permute-start | bytes 393224 | tf_op jit(solution)/shard_map/ppermute | solution.py:227
  50.3 5.6 %collective-permute-start.10 = (f32[64,512]{1,0:T(8,128)S(1)}, f32[64,512]{1,0:T(8,128)S(1)}, u32[]{:S(2)}, u32[]{:S(2)}) collective-permute-start(f32[64,512]{1,0:T(8,128)S(1)} %get-tuple-element.6), channel_id=1, source_target_pairs={{0,8},{8,16},{16,24},{1,9},{9,17},{17,25},{2,10},{10,18},{18,26},{... | collective-permute-start | bytes 393224 | tf_op jit(solution)/shard_map/ppermute | solution.py:227
  55.9 0.7 %slice.29 = f32[1,512]{1,0:T(1,128)S(1)} slice(f32[72,512]{1,0:T(8,128)} %shard_map.64.refs_0_), slice={[68:69], [0:512]} | slice | bytes 4096 | tf_op jit(solution)/shard_map/slice | solution.py:260
  56.6 9.2 %shard_map.66 = f32[1,64,512]{2,1,0:T(8,128)S(1)} custom-call(f32[72,512]{1,0:T(8,128)S(1)} %collective-permute-done.refs_0_, f32[72,512]{1,0:T(8,128)S(1)} %collective-permute-done.1.refs_1_, f32[72,512]{1,0:T(8,128)S(1)} %collective-permute-done.2.refs_2_, f32[72,512]{1,0:T(8,128)S(1)} %collective-permute-done.3.refs_3_, ...), custom_call_target="tpu_custom_call" | custom-call | flops 1207959552 | bytes 1327104 | tf_op jit(solution)/shard_map/pallas_call | solution.py:196
  65.8 0.0 collective-permute-done.9
  65.8 0.0 collective-permute-done.10
  65.8 0.7 %fusion.1 = f32[64,512]{1,0:T(8,128)} fusion(f32[64,512]{1,0:T(8,128)S(1)} %collective-permute-done.10, f32[64,512]{1,0:T(8,128)S(1)} %collective-permute-done.9, f32[1,64,512]{2,1,0:T(8,128)S(1)} %shard_map.66, f32[512]{0:T(512)S(1)} %bitcast.13), kind=kLoop, calls=%fused_computation.4 | loop fusion | flops 98304 | bytes 526336 | tf_op jit(solution)/shard_map/mul | solution.py:260
  (3 shorter events, 0.0 us)
Async XLA Ops:
  2.6 10.0 %collective-permute-start.4 = (f32[72,512]{1,0:T(8,128)}, f32[72,512]{1,0:T(8,128)S(1)}, u32[]{:S(2)}, u32[]{:S(2)}) collective-permute-start(f32[72,512]{1,0:T(8,128)} %shard_map.64.refs_0_), channel_id=1, source_target_pairs={{0,6},{1,7},{2,4},{3,5},{4,2},{5,3},{6,0},{7,1},{8,14},{9,15},{10,... | collective-permute-start | bytes 442376 | tf_op jit(solution)/shard_map/ppermute | solution.py:231
  7.7 12.8 %collective-permute-start.2 = (f32[72,512]{1,0:T(8,128)}, f32[72,512]{1,0:T(8,128)S(1)}, u32[]{:S(2)}, u32[]{:S(2)}) collective-permute-start(f32[72,512]{1,0:T(8,128)} %shard_map.64.refs_0_), channel_id=1, source_target_pairs={{0,4},{1,5},{2,6},{3,7},{4,0},{5,1},{6,2},{7,3},{8,12},{9,13},{10,... | collective-permute-start | bytes 442376 | tf_op jit(solution)/shard_map/ppermute | solution.py:231
  7.7 12.8 %collective-permute-start = (f32[72,512]{1,0:T(8,128)}, f32[72,512]{1,0:T(8,128)S(1)}, u32[]{:S(2)}, u32[]{:S(2)}) collective-permute-start(f32[72,512]{1,0:T(8,128)} %shard_map.64.refs_0_), channel_id=1, source_target_pairs={{0,2},{1,3},{2,0},{3,1},{4,6},{5,7},{6,4},{7,5},{8,10},{9,11},{10,... | collective-permute-start | bytes 442376 | tf_op jit(solution)/shard_map/ppermute | solution.py:231
  8.2 24.8 %collective-permute-start.8 = (f32[72,512]{1,0:T(8,128)}, f32[72,512]{1,0:T(8,128)S(1)}, u32[]{:S(2)}, u32[]{:S(2)}) collective-permute-start(f32[72,512]{1,0:T(8,128)} %shard_map.64.refs_0_), channel_id=1, source_target_pairs={{0,1},{1,0},{2,3},{3,2},{4,5},{5,4},{6,7},{7,6},{8,9},{9,8},{10,11... | collective-permute-start | bytes 442376 | tf_op jit(solution)/shard_map/ppermute | solution.py:231
  12.6 26.9 %collective-permute-start.5 = (f32[72,512]{1,0:T(8,128)S(1)}, f32[72,512]{1,0:T(8,128)S(1)}, u32[]{:S(2)}, u32[]{:S(2)}) collective-permute-start(f32[72,512]{1,0:T(8,128)S(1)} %collective-permute-done.4.refs_4_), channel_id=1, source_target_pairs={{0,1},{1,0},{2,3},{3,2},{4,5},{5,4},{6,7},{7,6},{8,9},{9,8},{10,11... | collective-permute-start | bytes 442376 | tf_op jit(solution)/shard_map/ppermute | solution.py:231
  20.5 19.1 %collective-permute-start.3 = (f32[72,512]{1,0:T(8,128)S(1)}, f32[72,512]{1,0:T(8,128)S(1)}, u32[]{:S(2)}, u32[]{:S(2)}) collective-permute-start(f32[72,512]{1,0:T(8,128)S(1)} %collective-permute-done.2.refs_2_), channel_id=1, source_target_pairs={{0,1},{1,0},{2,3},{3,2},{4,5},{5,4},{6,7},{7,6},{8,9},{9,8},{10,11... | collective-permute-start | bytes 442376 | tf_op jit(solution)/shard_map/ppermute | solution.py:231
  20.5 19.1 %collective-permute-start.1 = (f32[72,512]{1,0:T(8,128)S(1)}, f32[72,512]{1,0:T(8,128)S(1)}, u32[]{:S(2)}, u32[]{:S(2)}) collective-permute-start(f32[72,512]{1,0:T(8,128)S(1)} %collective-permute-done.refs_0_), channel_id=1, source_target_pairs={{0,1},{1,0},{2,3},{3,2},{4,5},{5,4},{6,7},{7,6},{8,9},{9,8},{10,11... | collective-permute-start | bytes 442376 | tf_op jit(solution)/shard_map/ppermute | solution.py:231
  21.7 5.6 %collective-permute-start.7 = (f32[8,512]{1,0:T(8,128)S(1)}, f32[8,512]{1,0:T(8,128)S(1)}, u32[]{:S(2)}, u32[]{:S(2)}) collective-permute-start(f32[8,512]{1,0:T(8,128)S(1)} %slice.25.refs_3_.refs_7_), channel_id=1, source_target_pairs={{8,0},{16,8},{24,16},{9,1},{17,9},{25,17},{10,2},{18,10},{26,18},{... | collective-permute-start | bytes 49160 | tf_op jit(solution)/shard_map/ppermute | solution.py:227
  27.3 5.6 %collective-permute-start.6 = (f32[8,512]{1,0:T(8,128)S(1)}, f32[8,512]{1,0:T(8,128)S(1)}, u32[]{:S(2)}, u32[]{:S(2)}) collective-permute-start(f32[8,512]{1,0:T(8,128)S(1)} %slice.25.refs_3_.refs_7_), channel_id=1, source_target_pairs={{0,8},{8,16},{16,24},{1,9},{9,17},{17,25},{2,10},{10,18},{18,26},{... | collective-permute-start | bytes 49160 | tf_op jit(solution)/shard_map/ppermute | solution.py:227
  33.0 0.9 %copy-start = (f32[72,512]{1,0:T(8,128)S(1)}, f32[72,512]{1,0:T(8,128)}, u32[]{:S(2)}) copy-start(f32[72,512]{1,0:T(8,128)} %shard_map.64.refs_0_) | copy-start | bytes 442372
  49.0 16.9 %collective-permute-start.9 = (f32[64,512]{1,0:T(8,128)S(1)}, f32[64,512]{1,0:T(8,128)S(1)}, u32[]{:S(2)}, u32[]{:S(2)}) collective-permute-start(f32[64,512]{1,0:T(8,128)S(1)} %get-tuple-element.5), channel_id=1, source_target_pairs={{8,0},{16,8},{24,16},{9,1},{17,9},{25,17},{10,2},{18,10},{26,18},{... | collective-permute-start | bytes 393224 | tf_op jit(solution)/shard_map/ppermute | solution.py:227
  50.3 15.6 %collective-permute-start.10 = (f32[64,512]{1,0:T(8,128)S(1)}, f32[64,512]{1,0:T(8,128)S(1)}, u32[]{:S(2)}, u32[]{:S(2)}) collective-permute-start(f32[64,512]{1,0:T(8,128)S(1)} %get-tuple-element.6), channel_id=1, source_target_pairs={{0,8},{8,16},{16,24},{1,9},{9,17},{17,25},{2,10},{10,18},{18,26},{... | collective-permute-start | bytes 393224 | tf_op jit(solution)/shard_map/ppermute | solution.py:227
